TPU v7x, 32 devices: a whole 2x2x4 slice. The times are simulated.
32 devices in a mesh: dp: 8 (over z, y), tensor: 4 (over x, core).
Axes of the slice: x: 2, y: 2, z: 4, core: 2. Of those that a mesh axis runs over, the one named last changes fastest.
Arguments:
- query: bfloat16 [16, 128, 8192], P('dp', None, 'tensor'), may hold values from -6 to 6
- image: bfloat16 [16, 512, 8192], P('dp', None, 'tensor'), may hold values from -6 to 6
- tiles: int32 [16], replicated, may hold values from 0 to 4, as said below
- image_slot: int32 [16], replicated, may hold values from 0 to 15, as said below
- key_weight_matrix: bfloat16 [8192, 1024], P('dp', 'tensor'), may hold values from -0.0625 to 0.0625
- value_weight_matrix: bfloat16 [8192, 1024], P('dp', 'tensor'), may hold values from -0.0625 to 0.0625
- query_gain: float32 [128], replicated, may hold values from 0.5 to 2
- key_gain: float32 [128], replicated, may hold values from 0.5 to 2
- gate: float32 [1], replicated, may hold values from 0.3 to 1.5
- cotangent: bfloat16 [16, 128, 8192], P('dp', None, 'tensor'), may hold values from -6 to 6
Outputs:
- context: bfloat16 [16, 128, 8192], P('dp', None, 'tensor')
- d_query: bfloat16 [16, 128, 8192], P('dp', None, 'tensor')
- d_w_key: float32 [8192, 1024], P('dp', 'tensor')
- d_w_value: float32 [8192, 1024], P('dp', 'tensor')
Inputs may be any that keep to these rules, and one draw needn't show every extreme that they name: Some sample has 4 tiles and some has none. image_slot is a permutation of the samples. Sample s sits at dp index s // 2; the image rows image_slot[s] sit at the same dp index or at the one that differs from it by half the dp axis, and of the two samples at one dp index at most one has its image at the other index.
All inputs are finite; a program needn't handle non-finite values.
Results may differ from a plain program's by a relative error of at most 0.02.
Values may be sent and summed in bfloat16 or wider, within the bound.
A program may use at most 192 MiB of HBM per device.

v0:
```python
import jax
import jax.numpy as jnp
from jax import lax
from jax.sharding import PartitionSpec as P

TILE = 128


EPS = 1e-06


def swapped(shard, axis, distance):
    return lax.ppermute(shard, axis, [(i, i ^ 1 << distance) for i in range(lax.axis_size(axis))])


def rms_factor(values):
    return lax.rsqrt(jnp.mean(values * values, axis=-1, keepdims=True) + EPS)


def norm_back(values, norm_multiplier, gain, grad):
    weighted = grad * gain
    inner = jnp.sum(weighted * values, axis=-1, keepdims=True)
    return (
        norm_multiplier * weighted
        - values * (norm_multiplier * norm_multiplier * norm_multiplier) * inner / values.shape[-1]
    )


def choose(flag, local, remote, index):
    mine = lax.dynamic_index_in_dim(local, index, 0, keepdims=False)
    theirs = lax.dynamic_index_in_dim(remote, index, 0, keepdims=False)
    return jnp.where(flag, mine, theirs)


def attend(q_norm, keys, vals, cot, count, ratio):
    text_rows, kv_local, group, head_dim = q_norm.shape
    scale = head_dim ** (-0.5)

    def tile_scores(index):
        key_tile = lax.dynamic_slice_in_dim(keys, index * TILE, TILE, 0)
        val_tile = lax.dynamic_slice_in_dim(vals, index * TILE, TILE, 0)
        raw = (
            jnp.einsum("tkgd,skd->kgts", q_norm, key_tile, preferred_element_type=jnp.float32)
            * scale
        )
        return (jnp.exp(raw), key_tile, val_tile)

    def forward(index, carry):
        total, accum = carry
        expo, key_tile, val_tile = tile_scores(index)
        total = total + jnp.sum(expo, axis=-1, keepdims=True)
        accum = accum + jnp.einsum(
            "kgts,skd->tkgd",
            expo.astype(jnp.bfloat16),
            val_tile,
            preferred_element_type=jnp.float32,
        )
        return (total, accum)

    start = (
        jnp.zeros((kv_local, group, text_rows, 1), jnp.float32),
        jnp.zeros((text_rows, kv_local, group, head_dim), jnp.float32),
    )
    total, accum = lax.fori_loop(0, count, forward, start)
    total = total + (count == 0).astype(jnp.float32)
    total_rows = jnp.transpose(total[..., 0], (2, 0, 1))[..., None]
    attended = accum / total_rows
    d_att = ratio * cot.astype(jnp.float32)
    d_att_b = d_att.astype(jnp.bfloat16)
    scaled_b = (d_att / total_rows).astype(jnp.bfloat16)
    delta = jnp.transpose(jnp.sum(d_att * attended, axis=-1), (1, 2, 0))[..., None]

    def backward(index, carry):
        d_qn, d_keys, d_vals = carry
        expo, key_tile, val_tile = tile_scores(index)
        d_prob = jnp.einsum("tkgd,skd->kgts", d_att_b, val_tile, preferred_element_type=jnp.float32)
        d_score = (expo / total * (d_prob - delta)).astype(jnp.bfloat16)
        d_qn = d_qn + scale * jnp.einsum(
            "kgts,skd->tkgd", d_score, key_tile, preferred_element_type=jnp.float32
        )
        key_part = scale * jnp.einsum(
            "kgts,tkgd->skd", d_score, q_norm, preferred_element_type=jnp.float32
        )
        val_part = jnp.einsum(
            "kgts,tkgd->skd",
            expo.astype(jnp.bfloat16),
            scaled_b,
            preferred_element_type=jnp.float32,
        )
        d_keys = lax.dynamic_update_slice_in_dim(d_keys, key_part, index * TILE, 0)
        d_vals = lax.dynamic_update_slice_in_dim(d_vals, val_part, index * TILE, 0)
        return (d_qn, d_keys, d_vals)

    start = (
        jnp.zeros((text_rows, kv_local, group, head_dim), jnp.float32),
        jnp.zeros(keys.shape, jnp.float32),
        jnp.zeros(vals.shape, jnp.float32),
    )
    d_qn, d_keys, d_vals = lax.fori_loop(0, count, backward, start)
    return (ratio * attended, d_qn, d_keys, d_vals)


def per_device(
    query,
    image,
    tiles,
    image_slot,
    key_weight_matrix,
    value_weight_matrix,
    query_gain,
    key_gain,
    gate,
    cotangent,
):
    head_dim = query_gain.shape[0]
    samp_local = query.shape[0]
    text_rows = query.shape[1]
    kv_cols = key_weight_matrix.shape[1]
    kv_local = kv_cols // head_dim
    group = query.shape[2] // kv_cols
    img_rows = image.shape[1]
    tile_total = img_rows // TILE
    ratio = jnp.tanh(gate[0])
    top_bit = (lax.axis_size("dp") // 2).bit_length() - 1
    rank = lax.axis_index("dp")
    first = rank * samp_local
    local_ids = first + jnp.arange(samp_local, dtype=jnp.int32)
    every = jnp.arange(tiles.shape[0], dtype=jnp.int32)
    match = image_slot[None, :] == local_ids[:, None]
    slot_sample = jnp.sum(jnp.where(match, every[None, :], 0), axis=1)
    home_tiles = lax.dynamic_slice_in_dim(tiles, first, samp_local)
    home_slot = lax.dynamic_slice_in_dim(image_slot, first, samp_local)
    key_rows, value_rows = (
        lax.all_gather(key_weight_matrix, "dp", axis=0, tiled=True),
        lax.all_gather(value_weight_matrix, "dp", axis=0, tiled=True),
    )
    w_both = jnp.concatenate([key_rows, value_rows], axis=1)
    width = w_both.shape[0]
    projected = []
    kept = []
    for slot in range(samp_local):
        proj_parts = []
        feat_parts = []
        for index in range(tile_total):
            part = image[slot, index * TILE : (index + 1) * TILE]
            full = lax.all_gather(part, "tensor", axis=1, tiled=True)
            proj_parts.append(jnp.dot(full, w_both, preferred_element_type=jnp.float32))
            feat_parts.append(full)
        projected.append(jnp.concatenate(proj_parts, axis=0))
        kept.append(feat_parts)
    projected = jnp.stack(projected)
    kraw = projected[..., :kv_cols].reshape(samp_local, img_rows, kv_local, head_dim)
    key_factor = rms_factor(kraw)
    keys = (kraw * key_factor * key_gain).astype(jnp.bfloat16)
    vals = (
        projected[..., kv_cols:]
        .astype(jnp.bfloat16)
        .reshape(samp_local, img_rows, kv_local, head_dim)
    )
    q_raw = query.astype(jnp.float32).reshape(samp_local, text_rows, kv_local, group, head_dim)
    q_factor = rms_factor(q_raw)
    q_norm = (q_raw * q_factor * query_gain).astype(jnp.bfloat16)
    cot = cotangent.reshape(samp_local, text_rows, kv_local, group, head_dim)
    far_keys, far_vals = swapped((keys, vals), "dp", top_bit)
    gated_rows, d_qn_rows, home_dk, home_dv = ([], [], [], [])
    for own in range(samp_local):
        slot = home_slot[own]
        near = slot // samp_local == rank
        index = slot % samp_local
        result = attend(
            q_norm[own],
            choose(near, keys, far_keys, index),
            choose(near, vals, far_vals, index),
            cot[own],
            home_tiles[own],
            ratio,
        )
        gated_rows.append(result[0])
        d_qn_rows.append(result[1])
        home_dk.append(result[2])
        home_dv.append(result[3])
    home_dk = jnp.stack(home_dk)
    home_dv = jnp.stack(home_dv)
    far_dk, far_dv = (
        swapped(home_dk.astype(jnp.bfloat16), "dp", top_bit).astype(home_dk.dtype),
        swapped(home_dv.astype(jnp.bfloat16), "dp", top_bit).astype(home_dv.dtype),
    )
    slot_dk, slot_dv = ([], [])
    for slot in range(samp_local):
        sample = slot_sample[slot]
        near = sample // samp_local == rank
        index = sample % samp_local
        slot_dk.append(choose(near, home_dk, far_dk, index))
        slot_dv.append(choose(near, home_dv, far_dv, index))
    gated_rows = jnp.stack(gated_rows)
    d_qn_rows = jnp.stack(d_qn_rows)
    slot_dk = jnp.stack(slot_dk)
    slot_dv = jnp.stack(slot_dv)
    context = gated_rows.astype(jnp.bfloat16).reshape(query.shape)
    d_query = (
        norm_back(q_raw, q_factor, query_gain, d_qn_rows).astype(jnp.bfloat16).reshape(query.shape)
    )
    grad_key_unnormed = norm_back(kraw, key_factor, key_gain, slot_dk).astype(jnp.bfloat16)
    grad_key_unnormed = grad_key_unnormed.reshape(samp_local, img_rows, kv_cols)
    d_vals = slot_dv.astype(jnp.bfloat16).reshape(samp_local, img_rows, kv_cols)
    d_both = jnp.concatenate([grad_key_unnormed, d_vals], axis=2)
    dims = (((0,), (0,)), ((), ()))
    grads = jnp.zeros((width, 2 * kv_cols), jnp.float32)
    for slot in range(samp_local):
        for index in range(tile_total):
            grad_tile = d_both[slot, index * TILE : (index + 1) * TILE]
            grads = grads + lax.dot_general(
                kept[slot][index], grad_tile, dims, preferred_element_type=jnp.float32
            )
    shares = lax.psum_scatter(
        grads.astype(jnp.bfloat16), "dp", scatter_dimension=0, tiled=True
    ).astype(jnp.float32)
    return (context, d_query, shares[:, :kv_cols], shares[:, kv_cols:])


def solution(mesh):
    placed = (
        P("dp", None, "tensor"),
        P("dp", None, "tensor"),
        P(),
        P(),
        P("dp", "tensor"),
        P("dp", "tensor"),
        P(),
        P(),
        P(),
        P("dp", None, "tensor"),
    )
    return jax.shard_map(
        per_device,
        mesh=mesh,
        in_specs=placed,
        out_specs=(
            P("dp", None, "tensor"),
            P("dp", None, "tensor"),
            P("dp", "tensor"),
            P("dp", "tensor"),
        ),
        check_vma=False,
    )
```

profile of v0, /device:TPU:0, one launch (start us, length us, event | category | flops | bytes accessed | tf_op | source)
XLA Modules:
  0.0 796.1 jit_solution(15346358365718973161)
XLA Ops:
  33.5 52.8 %all-gather.19.cloned.1.call-done = bf16[8192,256]{1,0:T(8,128)(2,1)} async-done(((bf16[1024,256]{1,0:T(8,128)(2,1)}), bf16[8192,256]{1,0:T(8,128)(2,1)}) %all-gather.19.cloned.1.call-update) | async-done | bytes 4194320 | tf_op jit(solution)/shard_map/all_gather | solution.py:134
  90.8 69.3 %all-gather.21.cloned.1.call-done = bf16[8192,256]{1,0:T(8,128)(2,1)} async-done(((bf16[1024,256]{1,0:T(8,128)(2,1)}), bf16[8192,256]{1,0:T(8,128)(2,1)}) %all-gather.21.cloned.1.call-update) | async-done | bytes 4194320 | tf_op jit(solution)/shard_map/all_gather | solution.py:135
  164.6 17.9 %all-gather.23.cloned.1.call-done = bf16[1,128,8192]{2,1,0:T(8,128)(2,1)} async-done(((bf16[1,128,2048]{2,1,0:T(8,128)(2,1)}), bf16[1,128,8192]{2,1,0:T(8,128)(2,1)}) %all-gather.23.cloned.1.call-update) | async-done | bytes 2097168 | tf_op jit(solution)/shard_map/all_gather | solution.py:146
  187.8 18.8 %all-gather.25.cloned.1.call-done = bf16[1,128,8192]{2,1,0:T(8,128)(2,1)} async-done(((bf16[1,128,2048]{2,1,0:T(8,128)(2,1)}), bf16[1,128,8192]{2,1,0:T(8,128)(2,1)}) %all-gather.25.cloned.1.call-update) | async-done | bytes 2097168 | tf_op jit(solution)/shard_map/all_gather | solution.py:146
  211.8 18.8 %all-gather.27.cloned.1.call-done = bf16[1,128,8192]{2,1,0:T(8,128)(2,1)} async-done(((bf16[1,128,2048]{2,1,0:T(8,128)(2,1)}), bf16[1,128,8192]{2,1,0:T(8,128)(2,1)}) %all-gather.27.cloned.1.call-update) | async-done | bytes 2097168 | tf_op jit(solution)/shard_map/all_gather | solution.py:146
  235.9 18.8 %all-gather.29.cloned.1.call-done = bf16[1,128,8192]{2,1,0:T(8,128)(2,1)} async-done(((bf16[1,128,2048]{2,1,0:T(8,128)(2,1)}), bf16[1,128,8192]{2,1,0:T(8,128)(2,1)}) %all-gather.29.cloned.1.call-update) | async-done | bytes 2097168 | tf_op jit(solution)/shard_map/all_gather | solution.py:146
  254.6 5.3 fusion.108
  260.0 18.8 %all-gather.35.cloned.1.call-done = bf16[1,128,8192]{2,1,0:T(8,128)(2,1)} async-done(((bf16[1,128,2048]{2,1,0:T(8,128)(2,1)}), bf16[1,128,8192]{2,1,0:T(8,128)(2,1)}) %all-gather.35.cloned.1.call-update) | async-done | bytes 2097168 | tf_op jit(solution)/shard_map/all_gather | solution.py:146
  278.8 6.2 fusion.117
  285.0 18.0 %all-gather.37.cloned.1.call-done = bf16[1,128,8192]{2,1,0:T(8,128)(2,1)} async-done(((bf16[1,128,2048]{2,1,0:T(8,128)(2,1)}), bf16[1,128,8192]{2,1,0:T(8,128)(2,1)}) %all-gather.37.cloned.1.call-update) | async-done | bytes 2097168 | tf_op jit(solution)/shard_map/all_gather | solution.py:146
  303.0 6.0 fusion.120
  309.0 18.2 %all-gather.33.cloned.1.call-done = bf16[1,128,8192]{2,1,0:T(8,128)(2,1)} async-done(((bf16[1,128,2048]{2,1,0:T(8,128)(2,1)}), bf16[1,128,8192]{2,1,0:T(8,128)(2,1)}) %all-gather.33.cloned.1.call-update) | async-done | bytes 2097168 | tf_op jit(solution)/shard_map/all_gather | solution.py:146
  327.2 6.0 fusion.114
  333.2 18.6 %all-gather.31.cloned.1.call-done = bf16[1,128,8192]{2,1,0:T(8,128)(2,1)} async-done(((bf16[1,128,2048]{2,1,0:T(8,128)(2,1)}), bf16[1,128,8192]{2,1,0:T(8,128)(2,1)}) %all-gather.31.cloned.1.call-update) | async-done | bytes 2097168 | tf_op jit(solution)/shard_map/all_gather | solution.py:146
  351.8 5.3 fusion.111
  383.7 14.1 %collective-permute-done.1 = bf16[2,512,2,128]{3,1,2,0:T(8,128)(2,1)} collective-permute-done((bf16[2,512,2,128]{3,1,2,0:T(8,128)(2,1)}, bf16[2,512,2,128]{3,1,2,0:T(8,128)(2,1)}, u32[]{:S(2)}, u32[]{:S(2)}) %collective-permute-start.1) | collective-permute-done | bytes 524320 | tf_op jit(solution)/shard_map/ppermute | solution.py:13
  399.8 8.6 %collective-permute-done = bf16[2,512,2,128]{3,1,2,0:T(8,128)(2,1)} collective-permute-done((bf16[2,512,2,128]{3,1,2,0:T(8,128)(2,1)}, bf16[2,512,2,128]{3,1,2,0:T(8,128)(2,1)}, u32[]{:S(2)}, u32[]{:S(2)}) %collective-permute-start) | collective-permute-done | bytes 524320 | tf_op jit(solution)/shard_map/ppermute | solution.py:13
  410.4 13.7 %while.53 = (s32[]{:T(128)}, f32[2,8,128,1]{2,3,1,0:T(1,128)S(1)}, f32[128,2,8,128]{0,3,2,1:T(8,128)S(1)}, s32[]{:T(128)}, bf16[512,2,128]{2,0,1:T(8,128)(2,1)},...) while((s32[]{:T(128)}, f32[2,8,128,1]{2,3,1,0:T(1,128)S(1)}, ...), condition=%wide.region_7.8_spmd, body=%wide.region_5.7_spmd.sunk | while | flops 135266304 | bytes 3834019 | solution.py:64
  425.3 11.6 %while.52 = (s32[]{:T(128)}, f32[2,8,128,1]{2,3,1,0:T(1,128)S(1)}, f32[128,2,8,128]{0,3,2,1:T(8,128)}, s32[]{:T(128)}, bf16[512,2,128]{2,0,1:T(8,128)(2,1)S(1)},...) while((s32[]{:T(128)}, f32[2,8,128,1]{2,3,1,0:T(1,128)S(1)}, ...), condition=%wide.region_4.5_spmd, body=%wide.region_2.0_spmd.sunk | while | flops 135266304 | bytes 3834019 | solution.py:64
  441.9 23.3 %while.55 = (s32[]{:T(128)}, f32[128,2,8,128]{0,3,2,1:T(8,128)S(1)}, f32[512,2,128]{2,0,1:T(8,128)}, bf16[512,2,128]{2,0,1:T(8,128)(2,1)S(1)}, s32[]{:T(128)}, /...) while((s32[]{:T(128)}, ...), condition=%wide.region_13.14_spmd, body=%wide.region_12.13_spmd.sunk | while | flops 337674240 | bytes 11485427 | solution.py:99
  467.4 19.4 %while.54 = (s32[]{:T(128)}, f32[128,2,8,128]{0,3,2,1:T(8,128)S(1)}, f32[512,2,128]{2,0,1:T(8,128)}, bf16[512,2,128]{2,0,1:T(8,128)(2,1)}, s32[]{:T(128)}, /*ind...) while((s32[]{:T(128)}, ...), condition=%wide.region_10.11_spmd, body=%wide.region_9.10_spmd.sunk | while | flops 337674240 | bytes 11485427 | solution.py:99
  509.0 9.5 %collective-permute-done.2 = bf16[2,512,2,128]{3,1,2,0:T(8,128)(2,1)} collective-permute-done((bf16[2,512,2,128]{3,1,2,0:T(8,128)(2,1)}, bf16[2,512,2,128]{3,1,2,0:T(8,128)(2,1)}, u32[]{:S(2)}, u32[]{:S(2)}) %collective-permute-start.2) | collective-permute-done | bytes 524320 | tf_op jit(solution)/shard_map/ppermute | solution.py:13
  521.9 7.6 collective-permute-done.3
  542.1 8.2 %fusion.71 = f32[512,8192]{1,0:T(8,128)} fusion(bf16[1,128,8192]{2,1,0:T(8,128)(2,1)S(1)} %copy-done.9, bf16[2,512,512]{2,1,0:T(8,128)(2,1)S(1)} %maximum_maximum_fusion), kind=kOutput, calls=%fused_computation.90 | convolution fusion | flops 1073741824 | bytes 19005440 | tf_op jit(solution)/shard_map/dot_general | solution.py:212
  550.3 8.1 %fusion.75 = f32[512,8192]{1,0:T(8,128)} fusion(bf16[1,128,8192]{2,1,0:T(8,128)(2,1)S(1)} %copy-done.10, bf16[2,512,512]{2,1,0:T(8,128)(2,1)S(1)} %maximum_maximum_fusion), kind=kOutput, calls=%fused_computation.94 | convolution fusion | flops 1073741824 | bytes 19005440 | tf_op jit(solution)/shard_map/dot_general | solution.py:212
  558.4 8.2 %fusion.79 = f32[512,8192]{1,0:T(8,128)} fusion(bf16[1,128,8192]{2,1,0:T(8,128)(2,1)S(1)} %copy-done.11, bf16[2,512,512]{2,1,0:T(8,128)(2,1)S(1)} %maximum_maximum_fusion), kind=kOutput, calls=%fused_computation.98 | convolution fusion | flops 1073741824 | bytes 19005440 | tf_op jit(solution)/shard_map/dot_general | solution.py:212
  566.6 8.1 %fusion.83 = f32[512,8192]{1,0:T(8,128)} fusion(bf16[1,128,8192]{2,1,0:T(8,128)(2,1)S(1)} %copy-done.8, bf16[2,512,512]{2,1,0:T(8,128)(2,1)S(1)} %maximum_maximum_fusion), kind=kOutput, calls=%fused_computation.102 | convolution fusion | flops 1073741824 | bytes 19005440 | tf_op jit(solution)/shard_map/dot_general | solution.py:212
  574.7 8.4 %fusion.87 = f32[512,8192]{1,0:T(8,128)} fusion(bf16[1,128,8192]{2,1,0:T(8,128)(2,1)S(1)} %copy-done.7, bf16[2,512,512]{2,1,0:T(8,128)(2,1)S(1)} %maximum_maximum_fusion), kind=kOutput, calls=%fused_computation.106 | convolution fusion | flops 1073741824 | bytes 19005440 | tf_op jit(solution)/shard_map/dot_general | solution.py:212
  583.1 8.2 %fusion.91 = f32[512,8192]{1,0:T(8,128)} fusion(bf16[1,128,8192]{2,1,0:T(8,128)(2,1)S(1)} %copy-done.6, bf16[2,512,512]{2,1,0:T(8,128)(2,1)S(1)} %maximum_maximum_fusion), kind=kOutput, calls=%fused_computation.110 | convolution fusion | flops 1073741824 | bytes 19005440 | tf_op jit(solution)/shard_map/dot_general | solution.py:212
  591.4 8.2 %fusion.95 = f32[512,8192]{1,0:T(8,128)} fusion(bf16[1,128,8192]{2,1,0:T(8,128)(2,1)S(1)} %copy-done.5, bf16[2,512,512]{2,1,0:T(8,128)(2,1)S(1)} %maximum_maximum_fusion), kind=kOutput, calls=%fused_computation.114 | convolution fusion | flops 1073741824 | bytes 19005440 | tf_op jit(solution)/shard_map/dot_general | solution.py:212
  599.5 39.9 %fusion.62 = bf16[8192,512]{0,1:T(8,128)(2,1)} fusion(f32[512,8192]{1,0:T(8,128)} %fusion.71, f32[512,8192]{1,0:T(8,128)} %fusion.75, f32[512,8192]{1,0:T(8,128)} %fusion.79, f32[512,8192]{1,0:T(8,128)} %fusion.83, f32[512,8192]{1,0:T(8,128)} %fusion.87, f32[512,8192]{1,0:T(8,128)} %fusion.95, f32[512,8192]{1,0:T(8,128)} %fusion.91, ...), kind=kOutput, calls=%fused_computation.77 | convolution fusion | flops 1107296256 | bytes 128057344 | tf_op jit(solution)/shard_map/dot_general | solution.py:212
  666.5 118.7 %reduce-scatter.2.cloned.1.call-done = bf16[1024,512]{0,1:T(8,128)(2,1)} async-done(((bf16[8192,512]{0,1:T(8,128)(2,1)}), bf16[1024,512]{0,1:T(8,128)(2,1)}) %reduce-scatter.2.cloned.1.call-update) | async-done | bytes 1048592 | tf_op jit(solution)/shard_map/reduce_scatter | solution.py:215
  (270 shorter events, 201.7 us)
Async XLA Ops:
  7.2 79.1 %all-gather.19.cloned.1.call-start = ((), (), s32[]{:S(2)}) async-start(), calls=%async_computation.1 | async-start | bytes 4718592 | tf_op jit(solution)/shard_map/all_gather | solution.py:134
  7.9 152.2 %all-gather.21.cloned.1.call-start = ((), (), s32[]{:S(2)}) async-start(), calls=%async_computation.2 | async-start | bytes 4718592 | tf_op jit(solution)/shard_map/all_gather | solution.py:135
  8.6 173.9 %all-gather.23.cloned.1.call-start = ((), (), s32[]{:S(2)}) async-start(), calls=%async_computation.4 | async-start | bytes 2621440 | tf_op jit(solution)/shard_map/all_gather | solution.py:146
  12.9 193.6 %all-gather.25.cloned.1.call-start = ((), (), s32[]{:S(2)}) async-start(), calls=%async_computation.5 | async-start | bytes 2621440 | tf_op jit(solution)/shard_map/all_gather | solution.py:146
  13.5 217.1 %all-gather.27.cloned.1.call-start = ((), (), s32[]{:S(2)}) async-start(), calls=%async_computation.6 | async-start | bytes 2621440 | tf_op jit(solution)/shard_map/all_gather | solution.py:146
  14.1 240.5 %all-gather.29.cloned.1.call-start = ((), (), s32[]{:S(2)}) async-start(), calls=%async_computation.7 | async-start | bytes 2621440 | tf_op jit(solution)/shard_map/all_gather | solution.py:146
  14.7 264.1 %all-gather.35.cloned.1.call-start = ((), (), s32[]{:S(2)}) async-start(), calls=%async_computation.10 | async-start | bytes 2621440 | tf_op jit(solution)/shard_map/all_gather | solution.py:146
  15.4 287.6 %all-gather.37.cloned.1.call-start = ((), (), s32[]{:S(2)}) async-start(), calls=%async_computation.11 | async-start | bytes 2621440 | tf_op jit(solution)/shard_map/all_gather | solution.py:146
  16.2 311.0 %all-gather.33.cloned.1.call-start = ((), (), s32[]{:S(2)}) async-start(), calls=%async_computation.9 | async-start | bytes 2621440 | tf_op jit(solution)/shard_map/all_gather | solution.py:146
  16.9 334.9 %all-gather.31.cloned.1.call-start = ((), (), s32[]{:S(2)}) async-start(), calls=%async_computation.8 | async-start | bytes 2621440 | tf_op jit(solution)/shard_map/all_gather | solution.py:146
  17.5 767.8 %reduce-scatter.2.cloned.1.call-start = ((), (), s32[]{:S(2)}) async-start(), calls=%async_computation.3 | async-start | bytes 9437184 | tf_op jit(solution)/shard_map/reduce_scatter | solution.py:215
  25.3 6.9 copy-start.34
  27.4 351.5 %copy-start.12 = (f32[1,128,2048]{1,2,0:T(8,128)}, f32[1,128,2048]{1,2,0:T(8,128)S(1)}, u32[]{:S(2)}) copy-start(f32[1,128,2048]{1,2,0:T(8,128)S(1)} %convert_multiply_fusion.1) | copy-start | bytes 3145732
  260.0 109.3 %copy-start = (f32[1,512,512]{2,1,0:T(8,128)}, f32[1,512,512]{2,1,0:T(8,128)S(1)}, u32[]{:S(2)}) copy-start(f32[1,512,512]{2,1,0:T(8,128)S(1)} %maximum_bitcast_fusion) | copy-start | bytes 3145732
  357.3 12.1 %copy-start.2 = (f32[1,512,512]{2,1,0:T(8,128)}, f32[1,512,512]{2,1,0:T(8,128)S(1)}, u32[]{:S(2)}) copy-start(f32[1,512,512]{2,1,0:T(8,128)S(1)} %maximum_bitcast_fusion.1) | copy-start | bytes 3145732
  359.4 10.0 %copy-start.36 = (f32[128]{0:T(128)S(1)}, f32[128]{0:T(128)}, u32[]{:S(2)}) copy-start(f32[128]{0:T(128)} %param.25) | copy-start | bytes 1540
  359.4 38.4 %collective-permute-start.1 = (bf16[2,512,2,128]{3,1,2,0:T(8,128)(2,1)}, bf16[2,512,2,128]{3,1,2,0:T(8,128)(2,1)}, u32[]{:S(2)}, u32[]{:S(2)}) collective-permute-start(bf16[2,512,2,128]{3,1,2,0:T(8,128)(2,1)} %copy_bitcast_fusion.2), channel_id=1, source_target_pairs={{0,16},{4,20},{8,24},{12,28},{16,0},{20,4},{24,8},{28,12},{1,17},{... | collective-permute-start | bytes 1572872 | tf_op jit(solution)/shard_map/ppermute | solution.py:13
  370.5 11.4 %copy-start.13 = (f32[1,128,2048]{1,2,0:T(8,128)S(1)}, f32[1,128,2048]{1,2,0:T(8,128)}, u32[]{:S(2)}) copy-start(f32[1,128,2048]{1,2,0:T(8,128)} %convert_multiply_fusion) | copy-start | bytes 3145732
  370.5 37.8 %collective-permute-start = (bf16[2,512,2,128]{3,1,2,0:T(8,128)(2,1)}, bf16[2,512,2,128]{3,1,2,0:T(8,128)(2,1)}, u32[]{:S(2)}, u32[]{:S(2)}) collective-permute-start(bf16[2,512,2,128]{3,1,2,0:T(8,128)(2,1)} %fusion.127), channel_id=1, source_target_pairs={{0,16},{4,20},{8,24},{12,28},{16,0},{20,4},{24,8},{28,12},{1,17},{... | collective-permute-start | bytes 1572872 | tf_op jit(solution)/shard_map/ppermute | solution.py:13
  488.9 29.6 %collective-permute-start.2 = (bf16[2,512,2,128]{3,1,2,0:T(8,128)(2,1)}, bf16[2,512,2,128]{3,1,2,0:T(8,128)(2,1)}, u32[]{:S(2)}, u32[]{:S(2)}) collective-permute-start(bf16[2,512,2,128]{3,1,2,0:T(8,128)(2,1)} %fusion.124), channel_id=1, source_target_pairs={{0,16},{4,20},{8,24},{12,28},{16,0},{20,4},{24,8},{28,12},{1,17},{... | collective-permute-start | bytes 1572872 | tf_op jit(solution)/shard_map/ppermute | solution.py:13
  504.9 14.7 %copy-start.15 = (f32[512,2,128]{2,0,1:T(8,128)S(1)}, f32[512,2,128]{2,0,1:T(8,128)}, u32[]{:S(2)}) copy-start(f32[512,2,128]{2,0,1:T(8,128)} %get-tuple-element.218) | copy-start | bytes 1572868
  504.9 14.7 %copy-start.16 = (f32[512,2,128]{2,0,1:T(8,128)S(1)}, f32[512,2,128]{2,0,1:T(8,128)}, u32[]{:S(2)}) copy-start(f32[512,2,128]{2,0,1:T(8,128)} %get-tuple-element.219) | copy-start | bytes 1572868
  506.0 13.8 %copy-start.1 = (f32[1,512,512]{2,1,0:T(8,128)S(1)}, f32[1,512,512]{2,1,0:T(8,128)}, u32[]{:S(2)}) copy-start(f32[1,512,512]{2,1,0:T(8,128)} %copy-done) | copy-start | bytes 3145732
  506.0 13.8 %copy-start.3 = (f32[1,512,512]{2,1,0:T(8,128)S(1)}, f32[1,512,512]{2,1,0:T(8,128)}, u32[]{:S(2)}) copy-start(f32[1,512,512]{2,1,0:T(8,128)} %copy-done.2) | copy-start | bytes 3145732
  506.0 23.5 %collective-permute-start.3 = (bf16[2,512,2,128]{3,1,2,0:T(8,128)(2,1)S(1)}, bf16[2,512,2,128]{3,1,2,0:T(8,128)(2,1)S(1)}, u32[]{:S(2)}, u32[]{:S(2)}) collective-permute-start(bf16[2,512,2,128]{3,1,2,0:T(8,128)(2,1)S(1)} %fusion.123), channel_id=1, source_target_pairs={{0,16},{4,20},{8,24},{12,28},{16,0},{20,4},{24,8},{28,12},{1,17},{... | collective-permute-start | bytes 1572872 | tf_op jit(solution)/shard_map/ppermute | solution.py:13
  519.9 9.7 %copy-start.21 = (bf16[512,2,128]{2,0,1:T(8,128)(2,1)S(1)}, bf16[512,2,128]{2,0,1:T(8,128)(2,1)}, u32[]{:S(2)}) copy-start(bf16[512,2,128]{2,0,1:T(8,128)(2,1)} %get-tuple-element.220) | copy-start | bytes 786436
  542.1 8.2 %copy-start.10 = (bf16[1,128,8192]{2,1,0:T(8,128)(2,1)S(1)}, bf16[1,128,8192]{2,1,0:T(8,128)(2,1)}, u32[]{:S(2)}) copy-start(bf16[1,128,8192]{2,1,0:T(8,128)(2,1)} %all-gather.33.cloned.1.call-done) | copy-start | bytes 6291460
  550.3 8.1 %copy-start.11 = (bf16[1,128,8192]{2,1,0:T(8,128)(2,1)S(1)}, bf16[1,128,8192]{2,1,0:T(8,128)(2,1)}, u32[]{:S(2)}) copy-start(bf16[1,128,8192]{2,1,0:T(8,128)(2,1)} %all-gather.31.cloned.1.call-done) | copy-start | bytes 6291460
  558.4 8.2 %copy-start.8 = (bf16[1,128,8192]{2,1,0:T(8,128)(2,1)S(1)}, bf16[1,128,8192]{2,1,0:T(8,128)(2,1)}, u32[]{:S(2)}) copy-start(bf16[1,128,8192]{2,1,0:T(8,128)(2,1)} %all-gather.29.cloned.1.call-done) | copy-start | bytes 6291460
  566.6 8.1 %copy-start.7 = (bf16[1,128,8192]{2,1,0:T(8,128)(2,1)S(1)}, bf16[1,128,8192]{2,1,0:T(8,128)(2,1)}, u32[]{:S(2)}) copy-start(bf16[1,128,8192]{2,1,0:T(8,128)(2,1)} %all-gather.27.cloned.1.call-done) | copy-start | bytes 6291460
  574.7 8.4 %copy-start.6 = (bf16[1,128,8192]{2,1,0:T(8,128)(2,1)S(1)}, bf16[1,128,8192]{2,1,0:T(8,128)(2,1)}, u32[]{:S(2)}) copy-start(bf16[1,128,8192]{2,1,0:T(8,128)(2,1)} %all-gather.25.cloned.1.call-done) | copy-start | bytes 6291460
  583.1 8.2 %copy-start.5 = (bf16[1,128,8192]{2,1,0:T(8,128)(2,1)S(1)}, bf16[1,128,8192]{2,1,0:T(8,128)(2,1)}, u32[]{:S(2)}) copy-start(bf16[1,128,8192]{2,1,0:T(8,128)(2,1)} %all-gather.23.cloned.1.call-done) | copy-start | bytes 6291460
  (27 other events, 82.2 us)
Sparse Core Ops, SparseCore 0:
  10.1 76.0 all-gather.18
  88.4 71.6 all-gather.20
  161.6 20.8 all-gather.22
  183.9 22.5 all-gather.24
  208.0 22.5 all-gather.26
  232.0 22.5 all-gather.28
  256.2 22.5 all-gather.34
  280.4 22.5 all-gather.36
  304.6 22.5 all-gather.32
  329.2 22.5 all-gather.30
  639.5 145.7 reduce-scatter.1
where the time goes:
time: 805 us; the launch traced here: 796 us
  waiting for transfers between devices  434 us (54%)
  matrix products  197 us (24%)
  local copies, waits for them, and re-layouts  79 us (10%)
  other arithmetic  40.1 us (5%)
  between operations  27.1 us (3%)
  loops' own time  12.9 us (2%)
    all_gather x8, waiting for transfers between devices, per_device(): full = lax.all_gather(part, 'tensor', axis=1, tiled=True)  148 us
    reduce_scatter x1, waiting for transfers between devices, per_device(): lax.psum_scatter(grads.astype(jnp.bfloat16), 'dp', scatter_dimension=0, t...  119 us
    dot_general x8, matrix products, per_device(): lax.dot_general(kept[slot][index], grad_tile, dims, preferred_element_typ...  97.2 us
    all_gather x1, waiting for transfers between devices, per_device(): lax.all_gather(value_weight_matrix, 'dp', axis=0, tiled=True)  69.3 us
    all_gather x1, waiting for transfers between devices, per_device(): lax.all_gather(key_weight_matrix, 'dp', axis=0, tiled=True)  52.8 us
    dot_general x8, matrix products, per_device(): proj_parts.append(jnp.dot(full, w_both, preferred_element_type=jnp.float32))  44.6 us
    ppermute x4, waiting for transfers between devices, swapped(): lax.ppermute(shard, axis, [(i, i ^ 1 << distance) for i in range(lax.axis...  39.7 us
    mul x8, local copies, waits for them, and re-layouts, norm_back(): values * (norm_multiplier * norm_multiplier * norm_multiplier) * inner  17.6 us
  transfers between devices with their start and end apart: 15, of which 15 were waited for; matrix products, arithmetic and copies ran while one was open for 16% of the time, Pallas kernels for 0%

commit v1 on v0

v1 whole, which is shorter than its diff:
```python
import functools

import jax
import jax.numpy as jnp
from jax import lax
from jax.experimental import pallas as pl
from jax.experimental.pallas import tpu as pltpu
from jax.sharding import PartitionSpec as P

TILE = 128


EPS = 1e-06


def swapped(shard, axis, distance):
    return lax.ppermute(shard, axis, [(i, i ^ 1 << distance) for i in range(lax.axis_size(axis))])


def rms_factor(values):
    return lax.rsqrt(jnp.mean(values * values, axis=-1, keepdims=True) + EPS)


def norm_back(values, norm_multiplier, gain, grad):
    weighted = grad * gain
    inner = jnp.sum(weighted * values, axis=-1, keepdims=True)
    return (
        norm_multiplier * weighted
        - values * (norm_multiplier * norm_multiplier * norm_multiplier) * inner / values.shape[-1]
    )


def attend_kernel(
    group, source, count, q_ref, cot_ref, kv_ref, gain_ref, ratio_ref, ctx_ref, dq_ref, dkv_ref
):
    own = pl.program_id(0)
    rows = kv_ref.shape[1]
    dim = kv_ref.shape[2] // 2
    text = q_ref.shape[1]
    scale = dim ** (-0.5)
    f32 = jnp.float32
    bf16 = jnp.bfloat16
    tiles = count[own]
    ratio = ratio_ref[0]
    empty = (tiles == 0).astype(f32)
    gain = gain_ref[...]
    keys = kv_ref[0, :, :dim]
    vals = kv_ref[0, :, dim:]
    keys_t = keys.T
    vals_t = vals.T
    at_once = 2 if group % 2 == 0 else 1
    valid = lax.broadcasted_iota(jnp.int32, (rows, at_once * text), 0) < tiles * TILE
    across = (((1,), (1,)), ((), ()))
    d_keys = jnp.zeros((rows, dim), f32)
    d_vals = jnp.zeros((rows, dim), f32)

    def load(ref, first):
        parts = [
            ref[0, :, (first + i) * dim : (first + i + 1) * dim].astype(f32).T
            for i in range(at_once)
        ]
        return jnp.concatenate(parts, axis=1)

    def store(ref, first, value):
        for i in range(at_once):
            part = value[:, i * text : (i + 1) * text].T
            ref[0, :, (first + i) * dim : (first + i + 1) * dim] = part.astype(bf16)

    for first in range(0, group, at_once):
        q_raw = load(q_ref, first)
        d_att = ratio * load(cot_ref, first)
        q_factor = lax.rsqrt(jnp.mean(q_raw * q_raw, axis=0, keepdims=True) + EPS)
        q_norm = (q_raw * q_factor * gain).astype(bf16)
        scores = jnp.dot(keys, q_norm, preferred_element_type=f32) * scale
        expo = jnp.where(valid, jnp.exp(scores), 0.0)
        total = jnp.sum(expo, axis=0, keepdims=True) + empty
        inverse = 1.0 / total
        weights_b = expo.astype(bf16)
        attended = jnp.dot(vals_t, weights_b, preferred_element_type=f32) * inverse
        store(ctx_ref, first, ratio * attended)
        d_att_b = d_att.astype(bf16)
        scaled_b = (d_att * inverse).astype(bf16)
        delta = jnp.sum(d_att * attended, axis=0, keepdims=True)
        d_prob = jnp.dot(vals, d_att_b, preferred_element_type=f32)
        d_score = (expo * inverse * (d_prob - delta)).astype(bf16)
        d_qn = scale * jnp.dot(keys_t, d_score, preferred_element_type=f32)
        weighted = d_qn * gain
        inner = jnp.sum(weighted * q_raw, axis=0, keepdims=True)
        cubed = q_factor * q_factor * q_factor
        store(dq_ref, first, q_factor * weighted - q_raw * (cubed * inner / dim))
        d_keys += lax.dot_general(d_score, q_norm, across, preferred_element_type=f32)
        d_vals += lax.dot_general(weights_b, scaled_b, across, preferred_element_type=f32)
    dkv_ref[0, :, :dim] = (scale * d_keys).astype(bf16)
    dkv_ref[0, :, dim:] = d_vals.astype(bf16)


def attend(query, cot, kv, source, count, gain, ratio, kv_local, head_dim):
    samples, text, cols = query.shape
    img_rows = kv.shape[1]
    group = cols // (kv_local * head_dim)
    per_head = pl.BlockSpec((1, text, group * head_dim), lambda s, k, *_: (s, 0, k))
    flops = 12 * samples * text * cols * img_rows
    return pl.pallas_call(
        functools.partial(attend_kernel, group),
        grid_spec=pltpu.PrefetchScalarGridSpec(
            num_scalar_prefetch=2,
            grid=(samples, kv_local),
            in_specs=[
                per_head,
                per_head,
                pl.BlockSpec(
                    (1, img_rows, 2 * head_dim), lambda s, k, source, count: (source[s], 0, k)
                ),
                pl.BlockSpec((head_dim, 1), lambda s, k, *_: (0, 0)),
                pl.BlockSpec(memory_space=pltpu.SMEM),
            ],
            out_specs=[
                per_head,
                per_head,
                pl.BlockSpec((1, img_rows, 2 * head_dim), lambda s, k, *_: (s, 0, k)),
            ],
        ),
        out_shape=[
            jax.ShapeDtypeStruct(query.shape, jnp.bfloat16),
            jax.ShapeDtypeStruct(query.shape, jnp.bfloat16),
            jax.ShapeDtypeStruct((samples, img_rows, kv.shape[2]), jnp.bfloat16),
        ],
        compiler_params=pltpu.CompilerParams(vmem_limit_bytes=40 * 1024 * 1024),
        cost_estimate=pl.CostEstimate(
            flops=flops, bytes_accessed=8 * query.size, transcendentals=samples * text * cols
        ),
    )(source, count, query, cot, kv, gain.reshape(head_dim, 1), ratio.reshape(1))


def gather_features(image):
    bits = (lax.axis_size("tensor") - 1).bit_length()
    blocks = {0: [image[slot] for slot in range(image.shape[0])]}
    for bit in reversed(range(bits)):
        arrived = {}
        for offset, parts in blocks.items():
            arrived[offset ^ 1 << bit] = [swapped(part, "tensor", bit) for part in parts]
        blocks.update(arrived)
    return blocks


def per_device(
    query,
    image,
    tiles,
    image_slot,
    key_weight_matrix,
    value_weight_matrix,
    query_gain,
    key_gain,
    gate,
    cotangent,
):
    head_dim = query_gain.shape[0]
    samp_local = query.shape[0]
    own_rows, kv_cols = key_weight_matrix.shape
    kv_local = kv_cols // head_dim
    img_rows = image.shape[1]
    image_cols = image.shape[2]
    ratio = jnp.tanh(gate[0])
    top_bit = (lax.axis_size("dp") // 2).bit_length() - 1
    rank = lax.axis_index("dp")
    place = lax.axis_index("tensor")
    first = rank * samp_local
    local_ids = first + jnp.arange(samp_local, dtype=jnp.int32)
    every = jnp.arange(tiles.shape[0], dtype=jnp.int32)
    match = image_slot[None, :] == local_ids[:, None]
    slot_sample = jnp.sum(jnp.where(match, every[None, :], 0), axis=1)
    home_tiles = lax.dynamic_slice_in_dim(tiles, first, samp_local)
    home_slot = lax.dynamic_slice_in_dim(image_slot, first, samp_local)
    slot_away = slot_sample // samp_local != rank
    home_away = home_slot // samp_local != rank
    source = jnp.where(home_away, samp_local, home_slot % samp_local)

    w_own = jnp.stack(
        [
            key_weight_matrix.reshape(own_rows, kv_local, head_dim),
            value_weight_matrix.reshape(own_rows, kv_local, head_dim),
        ],
        axis=2,
    ).reshape(own_rows, 2 * kv_cols)
    w_both = lax.all_gather(w_own, "dp", axis=0, tiled=True)
    width = w_both.shape[0]
    blocks = gather_features(image)
    projected = []
    for slot in range(samp_local):
        total = None
        for offset, parts in blocks.items():
            begin = (place ^ offset) * image_cols
            w_rows = lax.dynamic_slice_in_dim(w_both, begin, image_cols, 0)
            term = jnp.dot(parts[slot], w_rows, preferred_element_type=jnp.float32)
            total = term if total is None else total + term
        projected.append(total)
    projected = jnp.stack(projected).reshape(samp_local, img_rows, kv_local, 2, head_dim)
    kraw = projected[..., 0, :]
    key_factor = rms_factor(kraw)
    keys = kraw * key_factor * key_gain
    kv = jnp.stack([keys, projected[..., 1, :]], axis=3).astype(jnp.bfloat16)
    kv = kv.reshape(samp_local, img_rows, 2 * kv_cols)
    far_kv = swapped(
        lax.dynamic_index_in_dim(kv, jnp.argmax(slot_away), 0, keepdims=True), "dp", top_bit
    )
    context, d_query, home_dkv = attend(
        query,
        cotangent,
        jnp.concatenate([kv, far_kv], axis=0),
        source.astype(jnp.int32),
        home_tiles,
        query_gain,
        ratio,
        kv_local,
        head_dim,
    )
    far_dkv = swapped(
        lax.dynamic_index_in_dim(home_dkv, jnp.argmax(home_away), 0, keepdims=False), "dp", top_bit
    )
    slot_dkv = []
    for slot in range(samp_local):
        near = lax.dynamic_index_in_dim(home_dkv, slot_sample[slot] % samp_local, 0, keepdims=False)
        slot_dkv.append(jnp.where(slot_away[slot], far_dkv, near))
    slot_dkv = jnp.stack(slot_dkv).astype(jnp.float32)
    slot_dkv = slot_dkv.reshape(samp_local, img_rows, kv_local, 2, head_dim)
    d_kraw = norm_back(kraw, key_factor, key_gain, slot_dkv[..., 0, :])
    d_both = jnp.stack([d_kraw, slot_dkv[..., 1, :]], axis=3).astype(jnp.bfloat16)
    d_both = d_both.reshape(samp_local, img_rows, 2 * kv_cols)
    dims = (((0,), (0,)), ((), ()))
    grads = jnp.zeros((width, 2 * kv_cols), jnp.bfloat16)
    for offset, parts in blocks.items():
        total = None
        for slot in range(samp_local):
            term = lax.dot_general(
                parts[slot], d_both[slot], dims, preferred_element_type=jnp.float32
            )
            total = term if total is None else total + term
        grads = lax.dynamic_update_slice_in_dim(
            grads, total.astype(jnp.bfloat16), (place ^ offset) * image_cols, 0
        )
    shares = lax.psum_scatter(grads, "dp", scatter_dimension=0, tiled=True).astype(jnp.float32)
    shares = shares.reshape(own_rows, kv_local, 2, head_dim)
    return (
        context,
        d_query,
        shares[:, :, 0].reshape(own_rows, kv_cols),
        shares[:, :, 1].reshape(own_rows, kv_cols),
    )


def solution(mesh):
    placed = (
        P("dp", None, "tensor"),
        P("dp", None, "tensor"),
        P(),
        P(),
        P("dp", "tensor"),
        P("dp", "tensor"),
        P(),
        P(),
        P(),
        P("dp", None, "tensor"),
    )
    return jax.shard_map(
        per_device,
        mesh=mesh,
        in_specs=placed,
        out_specs=(
            P("dp", None, "tensor"),
            P("dp", None, "tensor"),
            P("dp", "tensor"),
            P("dp", "tensor"),
        ),
        check_vma=False,
    )
```

time: 805 us -> 425 us (0.53)
  matrix products: 197 us -> 46 us
  waiting for transfers between devices: 434 us -> 305 us
  local copies, waits for them, and re-layouts: 79 us -> 22.7 us
  other arithmetic: 40.1 us -> 7.67 us
  Pallas kernels: 0 us -> 14.6 us
  loops' own time: 12.9 us -> 0 us
    all_gather x10 -> x1, waiting for transfers between devices: 270 us -> 29.1 us  [per_device(): w_both = lax.all_gather(w_own, 'dp', axis=0, tiled=True)]
    dot_general x65 -> x16, matrix products: 197 us -> 46 us  [the longest x8 23.5 us: per_device(): lax.dot_general(parts[slot], d_both[slot], dims, preferred_element_type=j...]
    ppermute x4 -> x8, waiting for transfers between devices: 39.7 us -> 128 us  [swapped(): lax.ppermute(shard, axis, [(i, i ^ 1 << distance) for i in range(lax.axis...]
    reduce_scatter x1, waiting for transfers between devices: 119 us -> 148 us  [per_device(): lax.psum_scatter(grads, 'dp', scatter_dimension=0, tiled=True)]
    mul x16 -> x0, local copies, waits for them, and re-layouts: 27.2 us -> none  [the longest x8 17.6 us: norm_back(): values * (norm_multiplier * norm_multiplier * norm_multiplier) * inner]
    convert_element_type x10 -> x0, other arithmetic: 19.1 us -> none  [the longest x1 4.91 us: per_device(): norm_back(q_raw, q_factor, query_gain, d_qn_rows).astype(jnp.bfloat16)]
    pallas_call x0 -> x1, Pallas kernels: none -> 14.6 us  [attend(): pl.pallas_call(functools.partial(attend_kernel, group), grid_spec=pltpu.P...]
    another operation x4 -> x0, loops' own time: 12.9 us -> none  [the longest x2 6.53 us: attend(): d_qn, d_keys, d_vals = lax.fori_loop(0, count, backward, start)]
  transfers between devices with their start and end apart: 15 -> 10, of which waited for: 15 -> 6; matrix products, arithmetic and copies ran while one was open for 16% -> 7% of each run, Pallas kernels for 0% -> 0%
where the time goes in v1:
time: 425 us; the launch traced here: 424 us
  waiting for transfers between devices  305 us (72%)
  matrix products  46 us (11%)
  local copies, waits for them, and re-layouts  22.7 us (5%)
  between operations  22.7 us (5%)
  Pallas kernels  14.6 us (3%)
  other arithmetic  7.67 us (2%)
  starting transfers between devices  5.15 us (1%)
    reduce_scatter x1, waiting for transfers between devices, per_device(): lax.psum_scatter(grads, 'dp', scatter_dimension=0, tiled=True)  148 us
    ppermute x8, waiting for transfers between devices, swapped(): lax.ppermute(shard, axis, [(i, i ^ 1 << distance) for i in range(lax.axis...  128 us
    all_gather x1, waiting for transfers between devices, per_device(): w_both = lax.all_gather(w_own, 'dp', axis=0, tiled=True)  29.1 us
    dot_general x8, matrix products, per_device(): lax.dot_general(parts[slot], d_both[slot], dims, preferred_element_type=j...  23.5 us
    dot_general x8, matrix products, per_device(): term = jnp.dot(parts[slot], w_rows, preferred_element_type=jnp.float32)  22.5 us
    pallas_call x1, Pallas kernels, attend(): pl.pallas_call(functools.partial(attend_kernel, group), grid_spec=pltpu.P...  14.6 us
    unnamed x34, local copies, waits for them, and re-layouts  8.98 us
  transfers between devices with their start and end apart: 10, of which 6 were waited for; matrix products, arithmetic and copies ran while one was open for 7% of the time, Pallas kernels for 0%

profile of v1, /device:TPU:0, one launch (start us, length us, event | category | flops | bytes accessed | tf_op | source)
XLA Modules:
  0.0 423.7 jit_solution(15043348431973438634)
XLA Ops:
  10.9 4.8 %slice_bitcast_fusion.1 = (bf16[512,2048]{1,0:T(8,128)(2,1)}, bf16[512,2048]{1,0:T(8,128)(2,1)}) fusion(bf16[2,512,2048]{2,1,0:T(8,128)(2,1)} %param.11), kind=kLoop, calls=%fused_computation.18 | loop fusion | bytes 8388608 | tf_op jit(solution)/shard_map/squeeze | solution.py:137
  15.7 2.9 collective-permute-start.3
  19.1 46.1 %collective-permute-done.3 = bf16[512,2048]{1,0:T(8,128)(2,1)S(1)} collective-permute-done((bf16[512,2048]{1,0:T(8,128)(2,1)}, bf16[512,2048]{1,0:T(8,128)(2,1)S(1)}, u32[]{:S(2)}, u32[]{:S(2)}) %collective-permute-start.3) | collective-permute-done | bytes 2097184 | tf_op jit(solution)/shard_map/ppermute | solution.py:17
  68.3 41.1 %collective-permute-done = bf16[512,2048]{1,0:T(8,128)(2,1)} collective-permute-done((bf16[512,2048]{1,0:T(8,128)(2,1)}, bf16[512,2048]{1,0:T(8,128)(2,1)}, u32[]{:S(2)}, u32[]{:S(2)}) %collective-permute-start) | collective-permute-done | bytes 2097184 | tf_op jit(solution)/shard_map/ppermute | solution.py:17
  109.5 29.1 %all-gather.2.cloned.1.call-done = bf16[8192,512]{0,1:T(8,128)(2,1)} async-done(((bf16[1024,512]{0,1:T(8,128)(2,1)}), bf16[8192,512]{0,1:T(8,128)(2,1)}) %all-gather.2.cloned.1.call-update) | async-done | bytes 8388624 | tf_op jit(solution)/shard_map/all_gather | solution.py:186
  138.6 3.7 fusion.22
  142.3 3.0 fusion.24
  145.4 2.9 fusion.14
  148.3 2.9 fusion.16
  151.2 1.3 fusion.35
  152.5 2.9 fusion.41
  155.4 2.9 fusion.29
  158.3 2.9 fusion.38
  164.1 1.5 collective-permute-start.6
  169.2 20.0 %collective-permute-done.6 = bf16[1,512,512]{2,1,0:T(8,128)(2,1)} collective-permute-done((bf16[1,512,512]{2,1,0:T(8,128)(2,1)}, bf16[1,512,512]{2,1,0:T(8,128)(2,1)}, u32[]{:S(2)}, u32[]{:S(2)}) %collective-permute-start.6) | collective-permute-done | bytes 524320 | tf_op jit(solution)/shard_map/ppermute | solution.py:17
  190.4 14.6 %shard_map.129 = (bf16[2,128,2048]{2,1,0:T(8,128)(2,1)}, bf16[2,128,2048]{2,1,0:T(8,128)(2,1)}, bf16[2,512,512]{2,1,0:T(8,128)(2,1)S(1)}) custom-call(s32[2]{0:T(128)S(1)} %get-tuple-element.40.source, s32[2]{0:T(128)S(1)} %dynamic_slice.37.count, bf16[2,128,2048]{2,1,0:T(8,128)(2,1)S(1)} %copy-done, bf16[2,128,2048]{2,1,0:T(8,128)(2,1)S(1)} %copy-done.1, ...), custom_call_target="tpu_custom_call" | custom-call | flops 3221225472 | bytes 4194304 | tf_op jit(solution)/shard_map/pallas_call | solution.py:103
  210.0 20.8 %collective-permute-done.7 = bf16[512,512]{1,0:T(8,128)(2,1)S(1)} collective-permute-done((bf16[512,512]{1,0:T(8,128)(2,1)S(1)}, bf16[512,512]{1,0:T(8,128)(2,1)S(1)}, u32[]{:S(2)}, u32[]{:S(2)}) %collective-permute-start.7) | collective-permute-done | bytes 524320 | tf_op jit(solution)/shard_map/ppermute | solution.py:17
  231.5 2.5 bitcast_select_fusion
  235.2 2.0 copy-done.3
  237.2 1.3 fusion.66
  238.5 4.3 %broadcast_in_dim.26 = bf16[8192,512]{0,1:T(8,128)(2,1)} broadcast(bf16[]{:T(256)} %constant.91.clone.1), dimensions={} | broadcast | bytes 8388610 | tf_op jit(solution)/shard_map/broadcast_in_dim | solution.py:231
  242.7 2.5 fusion.1
  245.3 1.3 fusion.72
  246.5 2.9 fusion.73
  249.4 2.9 fusion.74
  252.3 4.3 %fusion.3 = bf16[8192,512]{0,1:T(8,128)(2,1)} fusion(bf16[8192,512]{0,1:T(8,128)(2,1)} %fusion.1, s32[]{:T(128)S(6)} %select_n.96, f32[512,2048]{1,0:T(8,128)S(1)} %fusion.72, bf16[512,512]{0,1:T(8,128)(2,1)S(1)} %bitcast.87, bf16[512,2048]{1,0:T(8,128)(2,1)} %collective-permute-done), kind=kOutput, calls=%fused_computation.7 | convolution fusion | flops 1075838976 | bytes 8912900 | tf_op jit(solution)/shard_map/dot_general | solution.py:235
  256.6 4.2 fusion.5
  260.8 4.2 fusion.7
  265.1 147.8 %reduce-scatter.2.cloned.1.call-done = bf16[1024,512]{0,1:T(8,128)(2,1)} async-done(((bf16[8192,512]{0,1:T(8,128)(2,1)}), bf16[1024,512]{0,1:T(8,128)(2,1)}) %reduce-scatter.2.cloned.1.call-update) | async-done | bytes 1048592 | tf_op jit(solution)/shard_map/reduce_scatter | solution.py:242
  412.8 1.4 fusion.68
  414.3 1.3 copy.67
  415.6 1.3 copy.68
  (72 shorter events, 13.6 us)
Async XLA Ops:
  7.2 131.4 %all-gather.2.cloned.1.call-start = ((), (), s32[]{:S(2)}) async-start(), calls=%async_computation.1 | async-start | bytes 9437184 | tf_op jit(solution)/shard_map/all_gather | solution.py:186
  10.8 54.5 %copy-start.11 = (s32[16]{0:T(128)S(1)}, s32[16]{0:T(128)}, u32[]{:S(2)}) copy-start(s32[16]{0:T(128)} %param.13) | copy-start | bytes 196
  10.8 402.0 %reduce-scatter.2.cloned.1.call-start = ((), (), s32[]{:S(2)}) async-start(), calls=%async_computation.2 | async-start | bytes 9437184 | tf_op jit(solution)/shard_map/reduce_scatter | solution.py:242
  15.7 49.6 %collective-permute-start.3 = (bf16[512,2048]{1,0:T(8,128)(2,1)}, bf16[512,2048]{1,0:T(8,128)(2,1)S(1)}, u32[]{:S(2)}, u32[]{:S(2)}) collective-permute-start(bf16[512,2048]{1,0:T(8,128)(2,1)} %get-tuple-element.43), channel_id=1, source_target_pairs={{0,2},{1,3},{2,0},{3,1},{4,6},{5,7},{6,4},{7,5},{8,10},{9,11},{10,... | collective-permute-start | bytes 6291464 | tf_op jit(solution)/shard_map/ppermute | solution.py:17
  18.6 90.9 %collective-permute-start = (bf16[512,2048]{1,0:T(8,128)(2,1)}, bf16[512,2048]{1,0:T(8,128)(2,1)}, u32[]{:S(2)}, u32[]{:S(2)}) collective-permute-start(bf16[512,2048]{1,0:T(8,128)(2,1)} %get-tuple-element.42), channel_id=1, source_target_pairs={{0,2},{1,3},{2,0},{3,1},{4,6},{5,7},{6,4},{7,5},{8,10},{9,11},{10,... | collective-permute-start | bytes 6291464 | tf_op jit(solution)/shard_map/ppermute | solution.py:17
  18.6 126.7 %collective-permute-start.4 = (bf16[512,2048]{1,0:T(8,128)(2,1)}, bf16[512,2048]{1,0:T(8,128)(2,1)}, u32[]{:S(2)}, u32[]{:S(2)}) collective-permute-start(bf16[512,2048]{1,0:T(8,128)(2,1)} %get-tuple-element.43), channel_id=1, source_target_pairs={{0,1},{1,0},{2,3},{3,2},{4,5},{5,4},{6,7},{7,6},{8,9},{9,8},{10,11... | collective-permute-start | bytes 6291464 | tf_op jit(solution)/shard_map/ppermute | solution.py:17
  18.6 129.6 %collective-permute-start.1 = (bf16[512,2048]{1,0:T(8,128)(2,1)}, bf16[512,2048]{1,0:T(8,128)(2,1)}, u32[]{:S(2)}, u32[]{:S(2)}) collective-permute-start(bf16[512,2048]{1,0:T(8,128)(2,1)} %get-tuple-element.42), channel_id=1, source_target_pairs={{0,1},{1,0},{2,3},{3,2},{4,5},{5,4},{6,7},{7,6},{8,9},{9,8},{10,11... | collective-permute-start | bytes 6291464 | tf_op jit(solution)/shard_map/ppermute | solution.py:17
  65.3 85.9 %copy-start.6 = (bf16[512,2048]{1,0:T(8,128)(2,1)}, bf16[512,2048]{1,0:T(8,128)(2,1)S(1)}, u32[]{:S(2)}) copy-start(bf16[512,2048]{1,0:T(8,128)(2,1)S(1)} %collective-permute-done.3) | copy-start | bytes 6291460
  65.3 87.2 %collective-permute-start.5 = (bf16[512,2048]{1,0:T(8,128)(2,1)S(1)}, bf16[512,2048]{1,0:T(8,128)(2,1)}, u32[]{:S(2)}, u32[]{:S(2)}) collective-permute-start(bf16[512,2048]{1,0:T(8,128)(2,1)S(1)} %collective-permute-done.3), channel_id=1, source_target_pairs={{0,1},{1,0},{2,3},{3,2},{4,5},{5,4},{6,7},{7,6},{8,9},{9,8},{10,11... | collective-permute-start | bytes 6291464 | tf_op jit(solution)/shard_map/ppermute | solution.py:17
  109.5 48.8 %collective-permute-start.2 = (bf16[512,2048]{1,0:T(8,128)(2,1)}, bf16[512,2048]{1,0:T(8,128)(2,1)}, u32[]{:S(2)}, u32[]{:S(2)}) collective-permute-start(bf16[512,2048]{1,0:T(8,128)(2,1)} %collective-permute-done), channel_id=1, source_target_pairs={{0,1},{1,0},{2,3},{3,2},{4,5},{5,4},{6,7},{7,6},{8,9},{9,8},{10,11... | collective-permute-start | bytes 6291464 | tf_op jit(solution)/shard_map/ppermute | solution.py:17
  138.6 3.7 copy-start.2
  138.6 6.7 %slice-start = ((s8[8388608]{0:T(1024)(128)(4,1)}), s8[4194304]{0:T(1024)(128)(4,1)S(1)}, s32[]{:S(2)}) async-start(s8[8388608]{0:T(1024)(128)(4,1)} %bitcast.112), calls=%async_computation.3 | async-start | bytes 8388608
  142.2 3.1 slice-start.1
  161.3 1.1 copy-start.9
  161.5 1.0 copy-start.4
  162.7 5.0 %copy-start.12 = (s32[16]{0:T(128)S(1)}, s32[16]{0:T(128)}, u32[]{:S(2)}) copy-start(s32[16]{0:T(128)} %param.12) | copy-start | bytes 196
  162.7 5.1 %copy-start.10 = (f32[128]{0:T(128)S(1)}, f32[128]{0:T(128)}, u32[]{:S(2)}) copy-start(f32[128]{0:T(128)} %param.16) | copy-start | bytes 1540
  163.3 27.1 %copy-start = (bf16[2,128,2048]{2,1,0:T(8,128)(2,1)S(1)}, bf16[2,128,2048]{2,1,0:T(8,128)(2,1)}, u32[]{:S(2)}) copy-start(bf16[2,128,2048]{2,1,0:T(8,128)(2,1)} %q_ref.1) | copy-start | bytes 3145732
  163.3 27.1 %copy-start.1 = (bf16[2,128,2048]{2,1,0:T(8,128)(2,1)S(1)}, bf16[2,128,2048]{2,1,0:T(8,128)(2,1)}, u32[]{:S(2)}) copy-start(bf16[2,128,2048]{2,1,0:T(8,128)(2,1)} %cot_ref.1) | copy-start | bytes 3145732
  164.1 25.1 %collective-permute-start.6 = (bf16[1,512,512]{2,1,0:T(8,128)(2,1)}, bf16[1,512,512]{2,1,0:T(8,128)(2,1)}, u32[]{:S(2)}, u32[]{:S(2)}) collective-permute-start(bf16[1,512,512]{2,1,0:T(8,128)(2,1)} %constant_dynamic-slice_fusion), channel_id=1, source_target_pairs={{0,16},{4,20},{8,24},{12,28},{16,0},{20,4},{24,8},{28,12},{1,17},{... | collective-permute-start | bytes 1572872 | tf_op jit(solution)/shard_map/ppermute | solution.py:17
  205.0 25.7 %collective-permute-start.7 = (bf16[512,512]{1,0:T(8,128)(2,1)S(1)}, bf16[512,512]{1,0:T(8,128)(2,1)S(1)}, u32[]{:S(2)}, u32[]{:S(2)}) collective-permute-start(bf16[512,512]{1,0:T(8,128)(2,1)S(1)} %dynamic-slice_bitcast_fusion), channel_id=1, source_target_pairs={{0,16},{4,20},{8,24},{12,28},{16,0},{20,4},{24,8},{28,12},{1,17},{... | collective-permute-start | bytes 1572872 | tf_op jit(solution)/shard_map/ppermute | solution.py:17
  230.7 0.8 copy-start.8
  231.5 2.9 copy-start.5
  235.0 2.2 copy-start.3
  242.7 2.5 copy-start.7
Sparse Core Ops, SparseCore 0:
  10.9 127.6 all-gather.1
  265.2 147.6 reduce-scatter.1

commit v2 on v1

--- a/solution.py
+++ b/solution.py
@@ -94,40 +94,45 @@
     dkv_ref[0, :, dim:] = d_vals.astype(bf16)
 
 
-def attend(query, cot, kv, source, count, gain, ratio, kv_local, head_dim):
+def attend(query, cot, kv, source, count, gain, ratio, head, kv_local):
     samples, text, cols = query.shape
     img_rows = kv.shape[1]
-    group = cols // (kv_local * head_dim)
-    per_head = pl.BlockSpec((1, text, group * head_dim), lambda s, k, *_: (s, 0, k))
-    flops = 12 * samples * text * cols * img_rows
+    head_dim = gain.shape[0]
+    head_cols = cols // kv_local
+    group = head_cols // head_dim
+    per_head = pl.BlockSpec((1, text, head_cols), lambda s, *_: (s, 0, head))
+    alone = pl.BlockSpec((1, text, head_cols), lambda s, *_: (s, 0, 0))
+    out = jax.ShapeDtypeStruct((samples, text, head_cols), jnp.bfloat16)
     return pl.pallas_call(
         functools.partial(attend_kernel, group),
         grid_spec=pltpu.PrefetchScalarGridSpec(
             num_scalar_prefetch=2,
-            grid=(samples, kv_local),
+            grid=(samples,),
             in_specs=[
                 per_head,
                 per_head,
                 pl.BlockSpec(
-                    (1, img_rows, 2 * head_dim), lambda s, k, source, count: (source[s], 0, k)
+                    (1, img_rows, 2 * head_dim), lambda s, source, count: (source[s], 0, 0)
                 ),
-                pl.BlockSpec((head_dim, 1), lambda s, k, *_: (0, 0)),
+                pl.BlockSpec((head_dim, 1), lambda s, *_: (0, 0)),
                 pl.BlockSpec(memory_space=pltpu.SMEM),
             ],
             out_specs=[
-                per_head,
-                per_head,
-                pl.BlockSpec((1, img_rows, 2 * head_dim), lambda s, k, *_: (s, 0, k)),
+                alone,
+                alone,
+                pl.BlockSpec((1, img_rows, 2 * head_dim), lambda s, *_: (s, 0, 0)),
             ],
         ),
         out_shape=[
-            jax.ShapeDtypeStruct(query.shape, jnp.bfloat16),
-            jax.ShapeDtypeStruct(query.shape, jnp.bfloat16),
-            jax.ShapeDtypeStruct((samples, img_rows, kv.shape[2]), jnp.bfloat16),
+            out,
+            out,
+            jax.ShapeDtypeStruct((samples, img_rows, 2 * head_dim), jnp.bfloat16),
         ],
-        compiler_params=pltpu.CompilerParams(vmem_limit_bytes=40 * 1024 * 1024),
+        compiler_params=pltpu.CompilerParams(vmem_limit_bytes=32 * 1024 * 1024),
         cost_estimate=pl.CostEstimate(
-            flops=flops, bytes_accessed=8 * query.size, transcendentals=samples * text * cols
+            flops=12 * samples * text * head_cols * img_rows,
+            bytes_accessed=8 * samples * text * head_cols,
+            transcendentals=samples * text * group * img_rows,
         ),
     )(source, count, query, cot, kv, gain.reshape(head_dim, 1), ratio.reshape(1))
 
@@ -176,76 +181,95 @@
     home_away = home_slot // samp_local != rank
     source = jnp.where(home_away, samp_local, home_slot % samp_local)
 
-    w_own = jnp.stack(
-        [
-            key_weight_matrix.reshape(own_rows, kv_local, head_dim),
-            value_weight_matrix.reshape(own_rows, kv_local, head_dim),
-        ],
-        axis=2,
-    ).reshape(own_rows, 2 * kv_cols)
-    w_both = lax.all_gather(w_own, "dp", axis=0, tiled=True)
-    width = w_both.shape[0]
+    source = source.astype(jnp.int32)
+    slot_sent = jnp.argmax(slot_away)
+    home_sent = jnp.argmax(home_away)
+
+    heads = range(kv_local)
+    w_heads = []
+    for head in heads:
+        cols = slice(head * head_dim, (head + 1) * head_dim)
+        w_own = jnp.concatenate([key_weight_matrix[:, cols], value_weight_matrix[:, cols]], axis=1)
+        w_heads.append(lax.all_gather(w_own, "dp", axis=0, tiled=True))
+    width = w_heads[0].shape[0]
     blocks = gather_features(image)
-    projected = []
-    for slot in range(samp_local):
-        total = None
+
+    def project(head):
+        projected = []
+        for slot in range(samp_local):
+            total = None
+            for offset, parts in blocks.items():
+                begin = (place ^ offset) * image_cols
+                w_rows = lax.dynamic_slice_in_dim(w_heads[head], begin, image_cols, 0)
+                term = jnp.dot(parts[slot], w_rows, preferred_element_type=jnp.float32)
+                total = term if total is None else total + term
+            projected.append(total)
+        projected = jnp.stack(projected)
+        kraw = projected[..., :head_dim]
+        key_factor = rms_factor(kraw)
+        keys = kraw * key_factor * key_gain
+        kv = jnp.concatenate([keys, projected[..., head_dim:]], axis=2).astype(jnp.bfloat16)
+        sent = lax.dynamic_index_in_dim(kv, slot_sent, 0, keepdims=True)
+        return kraw, key_factor, kv, swapped(sent, "dp", top_bit)
+
+    def weight_share(head, kraw, key_factor, home_dkv):
+        sent = lax.dynamic_index_in_dim(home_dkv, home_sent, 0, keepdims=False)
+        far_dkv = swapped(sent, "dp", top_bit)
+        slot_dkv = []
+        for slot in range(samp_local):
+            index = slot_sample[slot] % samp_local
+            near = lax.dynamic_index_in_dim(home_dkv, index, 0, keepdims=False)
+            slot_dkv.append(jnp.where(slot_away[slot], far_dkv, near))
+        slot_dkv = jnp.stack(slot_dkv).astype(jnp.float32)
+        d_kraw = norm_back(kraw, key_factor, key_gain, slot_dkv[..., :head_dim])
+        d_both = jnp.concatenate([d_kraw, slot_dkv[..., head_dim:]], axis=2).astype(jnp.bfloat16)
+        dims = (((0,), (0,)), ((), ()))
+        grads = jnp.zeros((width, 2 * head_dim), jnp.bfloat16)
         for offset, parts in blocks.items():
-            begin = (place ^ offset) * image_cols
-            w_rows = lax.dynamic_slice_in_dim(w_both, begin, image_cols, 0)
-            term = jnp.dot(parts[slot], w_rows, preferred_element_type=jnp.float32)
-            total = term if total is None else total + term
-        projected.append(total)
-    projected = jnp.stack(projected).reshape(samp_local, img_rows, kv_local, 2, head_dim)
-    kraw = projected[..., 0, :]
-    key_factor = rms_factor(kraw)
-    keys = kraw * key_factor * key_gain
-    kv = jnp.stack([keys, projected[..., 1, :]], axis=3).astype(jnp.bfloat16)
-    kv = kv.reshape(samp_local, img_rows, 2 * kv_cols)
-    far_kv = swapped(
-        lax.dynamic_index_in_dim(kv, jnp.argmax(slot_away), 0, keepdims=True), "dp", top_bit
-    )
-    context, d_query, home_dkv = attend(
-        query,
-        cotangent,
-        jnp.concatenate([kv, far_kv], axis=0),
-        source.astype(jnp.int32),
-        home_tiles,
-        query_gain,
-        ratio,
-        kv_local,
-        head_dim,
-    )
-    far_dkv = swapped(
-        lax.dynamic_index_in_dim(home_dkv, jnp.argmax(home_away), 0, keepdims=False), "dp", top_bit
-    )
-    slot_dkv = []
-    for slot in range(samp_local):
-        near = lax.dynamic_index_in_dim(home_dkv, slot_sample[slot] % samp_local, 0, keepdims=False)
-        slot_dkv.append(jnp.where(slot_away[slot], far_dkv, near))
-    slot_dkv = jnp.stack(slot_dkv).astype(jnp.float32)
-    slot_dkv = slot_dkv.reshape(samp_local, img_rows, kv_local, 2, head_dim)
-    d_kraw = norm_back(kraw, key_factor, key_gain, slot_dkv[..., 0, :])
-    d_both = jnp.stack([d_kraw, slot_dkv[..., 1, :]], axis=3).astype(jnp.bfloat16)
-    d_both = d_both.reshape(samp_local, img_rows, 2 * kv_cols)
-    dims = (((0,), (0,)), ((), ()))
-    grads = jnp.zeros((width, 2 * kv_cols), jnp.bfloat16)
-    for offset, parts in blocks.items():
-        total = None
-        for slot in range(samp_local):
-            term = lax.dot_general(
-                parts[slot], d_both[slot], dims, preferred_element_type=jnp.float32
+            total = None
+            for slot in range(samp_local):
+                term = lax.dot_general(
+                    parts[slot], d_both[slot], dims, preferred_element_type=jnp.float32
+                )
+                total = term if total is None else total + term
+            grads = lax.dynamic_update_slice_in_dim(
+                grads, total.astype(jnp.bfloat16), (place ^ offset) * image_cols, 0
             )
-            total = term if total is None else total + term
-        grads = lax.dynamic_update_slice_in_dim(
-            grads, total.astype(jnp.bfloat16), (place ^ offset) * image_cols, 0
+        return grads
+
+    context, d_query, shares = [], [], []
+    before = None
+    for head in heads:
+        if before is not None:
+            w_heads[head], home_dkv = lax.optimization_barrier((w_heads[head], before[2]))
+            before = (before[0], before[1], home_dkv)
+        kraw, key_factor, kv, far_kv = project(head)
+        q_in = query
+        if before is not None:
+            grads, q_in = lax.optimization_barrier((weight_share(head - 1, *before), query))
+            shares.append(lax.psum_scatter(grads, "dp", scatter_dimension=0, tiled=True))
+        ctx, d_q, home_dkv = attend(
+            q_in,
+            cotangent,
+            jnp.concatenate([kv, far_kv], axis=0),
+            source,
+            home_tiles,
+            query_gain,
+            ratio,
+            head,
+            kv_local,
         )
-    shares = lax.psum_scatter(grads, "dp", scatter_dimension=0, tiled=True).astype(jnp.float32)
-    shares = shares.reshape(own_rows, kv_local, 2, head_dim)
+        context.append(ctx)
+        d_query.append(d_q)
+        before = (kraw, key_factor, home_dkv)
+    grads = weight_share(kv_local - 1, *before)
+    shares.append(lax.psum_scatter(grads, "dp", scatter_dimension=0, tiled=True))
+    shares = [share.astype(jnp.float32) for share in shares]
     return (
-        context,
-        d_query,
-        shares[:, :, 0].reshape(own_rows, kv_cols),
-        shares[:, :, 1].reshape(own_rows, kv_cols),
+        jnp.concatenate(context, axis=2),
+        jnp.concatenate(d_query, axis=2),
+        jnp.concatenate([share[:, :head_dim] for share in shares], axis=1),
+        jnp.concatenate([share[:, head_dim:] for share in shares], axis=1),
     )
 
 

time: 425 us -> 429 us (level)
  waiting for transfers between devices: 305 us -> 251 us
  matrix products: 46 us -> 73.6 us
  local copies, waits for them, and re-layouts: 22.7 us -> 44.4 us
  other arithmetic: 7.67 us -> 15.3 us
    reduce_scatter x1 -> x2, waiting for transfers between devices: 148 us -> 85.8 us  [per_device(): lax.psum_scatter(grads, 'dp', scatter_dimension=0, tiled=True)]
    ppermute x8 -> x10, waiting for transfers between devices: 128 us -> 165 us  [swapped(): lax.ppermute(shard, axis, [(i, i ^ 1 << distance) for i in range(lax.axis...]
    all_gather x1 -> x2, waiting for transfers between devices: 29.1 us -> 0.11 us  [per_device(): w_heads.append(lax.all_gather(w_own, 'dp', axis=0, tiled=True))]
    dot_general x16 -> x32, matrix products: 46 us -> 73.6 us  [the longest x16 41.4 us: weight_share(): lax.dot_general(parts[slot], d_both[slot], dims, preferred_element_type=j...]
    convert_element_type x1 -> x8, local copies, waits for them, and re-layouts: 0.54 us -> 16.5 us  [weight_share(): total.astype(jnp.bfloat16)]
    dynamic_update_slice x0 -> x8, local copies, waits for them, and re-layouts: none -> 8.52 us  [weight_share(): lax.dynamic_update_slice_in_dim(grads, total.astype(jnp.bfloat16), (place...]
    concatenate x0 -> x10, other arithmetic: none -> 6.09 us  [the longest x2 1.7 us: per_device(): jnp.concatenate([key_weight_matrix[:, cols], value_weight_matrix[:, cols]...]
    another operation x0 -> x2, local copies, waits for them, and re-layouts: none -> 4.49 us
  transfers between devices with their start and end apart: 10 -> 14, of which waited for: 6 -> 8; matrix products, arithmetic and copies ran while one was open for 7% -> 19% of each run, Pallas kernels for 0% -> 3%
where the time goes in v2:
time: 429 us; the launch traced here: 428 us
  waiting for transfers between devices  251 us (59%)
  matrix products  73.6 us (17%)
  local copies, waits for them, and re-layouts  44.4 us (10%)
  between operations  22.9 us (5%)
  other arithmetic  15.3 us (4%)
  Pallas kernels  14.3 us (3%)
  starting transfers between devices  6.75 us (2%)
    ppermute x10, waiting for transfers between devices, swapped(): lax.ppermute(shard, axis, [(i, i ^ 1 << distance) for i in range(lax.axis...  165 us
    reduce_scatter x2, waiting for transfers between devices, per_device(): lax.psum_scatter(grads, 'dp', scatter_dimension=0, tiled=True)  85.8 us
    dot_general x16, matrix products, weight_share(): lax.dot_general(parts[slot], d_both[slot], dims, preferred_element_type=j...  41.4 us
    dot_general x16, matrix products, project(): term = jnp.dot(parts[slot], w_rows, preferred_element_type=jnp.float32)  32.1 us
    convert_element_type x8, local copies, waits for them, and re-layouts, weight_share(): total.astype(jnp.bfloat16)  16.5 us
    pallas_call x2, Pallas kernels, attend(): pl.pallas_call(functools.partial(attend_kernel, group), grid_spec=pltpu.P...  14.3 us
  transfers between devices with their start and end apart: 14, of which 8 were waited for; matrix products, arithmetic and copies ran while one was open for 19% of the time, Pallas kernels for 3%

profile of v2, /device:TPU:0, one launch (start us, length us, event | category | flops | bytes accessed | tf_op | source)
XLA Modules:
  0.0 428.3 jit_solution(4245691097611353399)
XLA Ops:
  10.3 4.8 %slice_bitcast_fusion.1 = (bf16[512,2048]{1,0:T(8,128)(2,1)}, bf16[512,2048]{1,0:T(8,128)(2,1)}) fusion(bf16[2,512,2048]{2,1,0:T(8,128)(2,1)} %param.11), kind=kLoop, calls=%fused_computation.27 | loop fusion | bytes 8388608 | tf_op jit(solution)/shard_map/squeeze | solution.py:142
  15.1 2.9 collective-permute-start
  18.1 46.6 %collective-permute-done = bf16[512,2048]{1,0:T(8,128)(2,1)S(1)} collective-permute-done((bf16[512,2048]{1,0:T(8,128)(2,1)}, bf16[512,2048]{1,0:T(8,128)(2,1)S(1)}, u32[]{:S(2)}, u32[]{:S(2)}) %collective-permute-start) | collective-permute-done | bytes 2097184 | tf_op jit(solution)/shard_map/ppermute | solution.py:17
  66.1 42.9 %collective-permute-done.3 = bf16[512,2048]{1,0:T(8,128)(2,1)} collective-permute-done((bf16[512,2048]{1,0:T(8,128)(2,1)}, bf16[512,2048]{1,0:T(8,128)(2,1)}, u32[]{:S(2)}, u32[]{:S(2)}) %collective-permute-start.3) | collective-permute-done | bytes 2097184 | tf_op jit(solution)/shard_map/ppermute | solution.py:17
  111.0 2.7 fusion.42
  117.2 2.5 fusion.21
  120.8 2.7 convolution_add_fusion.16
  129.1 2.9 collective-permute-start.6
  140.0 21.7 %collective-permute-done.6 = bf16[1,512,256]{2,1,0:T(8,128)(2,1)S(1)} collective-permute-done((bf16[1,512,256]{2,1,0:T(8,128)(2,1)S(1)}, bf16[1,512,256]{2,1,0:T(8,128)(2,1)S(1)}, u32[]{:S(2)}, u32[]{:S(2)}) %collective-permute-start.6) | collective-permute-done | bytes 262176 | tf_op jit(solution)/shard_map/ppermute | solution.py:17
  163.0 7.0 %shard_map.129 = (bf16[2,128,1024]{2,1,0:T(8,128)(2,1)S(1)}, bf16[2,128,1024]{2,1,0:T(8,128)(2,1)S(1)}, bf16[2,512,256]{2,1,0:T(8,128)(2,1)S(1)}) custom-call(s32[2]{0:T(128)S(1)} %get-tuple-element.32.source, s32[2]{0:T(128)S(1)} %dynamic_slice.65.count, bf16[2,128,2048]{2,1,0:T(8,128)(2,1)S(1)} %copy-done, bf16[2,128,2048]{2,1,0:T(8,128)(2,1)S(1)} %copy-done.1, ...), custom_call_target="tpu_custom_call" | custom-call | flops 1610612736 | bytes 2097152 | tf_op jit(solution)/shard_map/pallas_call | solution.py:106
  170.8 13.5 %collective-permute-done.7 = bf16[512,256]{1,0:T(8,128)(2,1)S(1)} collective-permute-done((bf16[512,256]{1,0:T(8,128)(2,1)S(1)}, bf16[512,256]{1,0:T(8,128)(2,1)S(1)}, u32[]{:S(2)}, u32[]{:S(2)}) %collective-permute-start.7) | collective-permute-done | bytes 262176 | tf_op jit(solution)/shard_map/ppermute | solution.py:17
  189.9 2.3 fusion.71
  192.2 3.3 fusion.14
  197.8 2.3 fusion.72
  200.1 3.3 fusion.15
  205.7 2.5 fusion.73
  212.2 3.9 fusion.17
  224.8 2.7 fusion.32
  231.6 2.5 fusion.19
  235.1 2.3 convolution_add_fusion.10
  237.4 2.3 convolution_add_fusion.9
  239.8 2.3 fusion.18
  242.7 28.2 %collective-permute-done.8 = bf16[1,512,256]{2,1,0:T(8,128)(2,1)S(1)} collective-permute-done((bf16[1,512,256]{2,1,0:T(8,128)(2,1)S(1)}, bf16[1,512,256]{2,1,0:T(8,128)(2,1)S(1)}, u32[]{:S(2)}, u32[]{:S(2)}) %collective-permute-start.8) | collective-permute-done | bytes 262176 | tf_op jit(solution)/shard_map/ppermute | solution.py:17
  271.0 7.2 %shard_map.130 = (bf16[2,128,1024]{2,1,0:T(8,128)(2,1)S(1)}, bf16[2,128,1024]{2,1,0:T(8,128)(2,1)S(1)}, bf16[2,512,256]{2,1,0:T(8,128)(2,1)S(1)}) custom-call(s32[2]{0:T(128)S(1)} %get-tuple-element.32.source, s32[2]{0:T(128)S(1)} %dynamic_slice.65.count, bf16[2,128,2048]{2,1,0:T(8,128)(2,1)S(1)} %copy-done, bf16[2,128,2048]{2,1,0:T(8,128)(2,1)S(1)} %copy-done.2, ...), custom_call_target="tpu_custom_call" | custom-call | flops 1610612736 | bytes 2097152 | tf_op jit(solution)/shard_map/pallas_call | solution.py:106
  278.4 12.2 %collective-permute-done.9 = bf16[512,256]{1,0:T(8,128)(2,1)S(1)} collective-permute-done((bf16[512,256]{1,0:T(8,128)(2,1)S(1)}, bf16[512,256]{1,0:T(8,128)(2,1)S(1)}, u32[]{:S(2)}, u32[]{:S(2)}) %collective-permute-start.9) | collective-permute-done | bytes 262176 | tf_op jit(solution)/shard_map/ppermute | solution.py:17
  293.8 2.3 fusion.75
  296.1 3.3 fusion.10
  301.7 2.6 fusion.76
  304.4 3.3 fusion.11
  309.9 2.5 fusion.77
  316.4 2.5 fusion.74
  332.7 85.8 %reduce-scatter.5.cloned.1.call-done = bf16[1024,256]{1,0:T(8,128)(2,1)} async-done(((bf16[8192,256]{1,0:T(8,128)(2,1)}), bf16[1024,256]{1,0:T(8,128)(2,1)}) %reduce-scatter.5.cloned.1.call-update) | async-done | bytes 524304 | tf_op jit(solution)/shard_map/reduce_scatter | solution.py:266
  (138 shorter events, 75.3 us)
Async XLA Ops:
  7.2 103.8 %all-gather.3.cloned.1.call-start = ((), (), s32[]{:S(2)}) async-start(), calls=%async_computation.2 | async-start | bytes 4718592 | tf_op jit(solution)/shard_map/all_gather | solution.py:193
  9.3 160.8 %all-gather.5.cloned.1.call-start = ((), (), s32[]{:S(2)}) async-start(), calls=%async_computation.3 | async-start | bytes 4718592 | tf_op jit(solution)/shard_map/all_gather | solution.py:193
  10.3 55.0 %copy-start.21 = (s32[16]{0:T(128)S(1)}, s32[16]{0:T(128)}, u32[]{:S(2)}) copy-start(s32[16]{0:T(128)} %param.13) | copy-start | bytes 196
  10.3 321.3 %reduce-scatter.3.cloned.1.call-start = ((), (), s32[]{:S(2)}) async-start(), calls=%async_computation.4 | async-start | bytes 4718592 | tf_op jit(solution)/shard_map/reduce_scatter | solution.py:250
  15.1 49.6 %collective-permute-start = (bf16[512,2048]{1,0:T(8,128)(2,1)}, bf16[512,2048]{1,0:T(8,128)(2,1)S(1)}, u32[]{:S(2)}, u32[]{:S(2)}) collective-permute-start(bf16[512,2048]{1,0:T(8,128)(2,1)} %get-tuple-element.34), channel_id=1, source_target_pairs={{0,2},{1,3},{2,0},{3,1},{4,6},{5,7},{6,4},{7,5},{8,10},{9,11},{10,... | collective-permute-start | bytes 6291464 | tf_op jit(solution)/shard_map/ppermute | solution.py:17
  18.1 90.9 %collective-permute-start.3 = (bf16[512,2048]{1,0:T(8,128)(2,1)}, bf16[512,2048]{1,0:T(8,128)(2,1)}, u32[]{:S(2)}, u32[]{:S(2)}) collective-permute-start(bf16[512,2048]{1,0:T(8,128)(2,1)} %get-tuple-element.35), channel_id=1, source_target_pairs={{0,2},{1,3},{2,0},{3,1},{4,6},{5,7},{6,4},{7,5},{8,10},{9,11},{10,... | collective-permute-start | bytes 6291464 | tf_op jit(solution)/shard_map/ppermute | solution.py:17
  18.1 96.8 %collective-permute-start.1 = (bf16[512,2048]{1,0:T(8,128)(2,1)}, bf16[512,2048]{1,0:T(8,128)(2,1)}, u32[]{:S(2)}, u32[]{:S(2)}) collective-permute-start(bf16[512,2048]{1,0:T(8,128)(2,1)} %get-tuple-element.34), channel_id=1, source_target_pairs={{0,1},{1,0},{2,3},{3,2},{4,5},{5,4},{6,7},{7,6},{8,9},{9,8},{10,11... | collective-permute-start | bytes 6291464 | tf_op jit(solution)/shard_map/ppermute | solution.py:17
  64.7 49.0 %copy-start.7 = (bf16[512,2048]{1,0:T(8,128)(2,1)}, bf16[512,2048]{1,0:T(8,128)(2,1)S(1)}, u32[]{:S(2)}) copy-start(bf16[512,2048]{1,0:T(8,128)(2,1)S(1)} %collective-permute-done) | copy-start | bytes 6291460
  64.7 52.5 %collective-permute-start.2 = (bf16[512,2048]{1,0:T(8,128)(2,1)S(1)}, bf16[512,2048]{1,0:T(8,128)(2,1)}, u32[]{:S(2)}, u32[]{:S(2)}) collective-permute-start(bf16[512,2048]{1,0:T(8,128)(2,1)S(1)} %collective-permute-done), channel_id=1, source_target_pairs={{0,1},{1,0},{2,3},{3,2},{4,5},{5,4},{6,7},{7,6},{8,9},{9,8},{10,11... | collective-permute-start | bytes 6291464 | tf_op jit(solution)/shard_map/ppermute | solution.py:17
  64.7 58.8 %collective-permute-start.4 = (bf16[512,2048]{1,0:T(8,128)(2,1)}, bf16[512,2048]{1,0:T(8,128)(2,1)}, u32[]{:S(2)}, u32[]{:S(2)}) collective-permute-start(bf16[512,2048]{1,0:T(8,128)(2,1)} %get-tuple-element.35), channel_id=1, source_target_pairs={{0,1},{1,0},{2,3},{3,2},{4,5},{5,4},{6,7},{7,6},{8,9},{9,8},{10,11... | collective-permute-start | bytes 6291464 | tf_op jit(solution)/shard_map/ppermute | solution.py:17
  108.9 16.9 %collective-permute-start.5 = (bf16[512,2048]{1,0:T(8,128)(2,1)}, bf16[512,2048]{1,0:T(8,128)(2,1)}, u32[]{:S(2)}, u32[]{:S(2)}) collective-permute-start(bf16[512,2048]{1,0:T(8,128)(2,1)} %collective-permute-done.3), channel_id=1, source_target_pairs={{0,1},{1,0},{2,3},{3,2},{4,5},{5,4},{6,7},{7,6},{8,9},{9,8},{10,11... | collective-permute-start | bytes 6291464 | tf_op jit(solution)/shard_map/ppermute | solution.py:17
  111.0 3.1 copy-start.12
  117.2 2.8 copy-start.3
  128.2 10.2 %copy-start.22 = (s32[16]{0:T(128)S(1)}, s32[16]{0:T(128)}, u32[]{:S(2)}) copy-start(s32[16]{0:T(128)} %param.12) | copy-start | bytes 196
  128.2 10.3 %copy-start.20 = (f32[128]{0:T(128)S(1)}, f32[128]{0:T(128)}, u32[]{:S(2)}) copy-start(f32[128]{0:T(128)} %param.16) | copy-start | bytes 1540
  128.2 33.5 %copy-start = (bf16[2,128,2048]{2,1,0:T(8,128)(2,1)S(1)}, bf16[2,128,2048]{2,1,0:T(8,128)(2,1)}, u32[]{:S(2)}) copy-start(bf16[2,128,2048]{2,1,0:T(8,128)(2,1)} %q_ref.2) | copy-start | bytes 3145732
  129.1 32.6 %collective-permute-start.6 = (bf16[1,512,256]{2,1,0:T(8,128)(2,1)S(1)}, bf16[1,512,256]{2,1,0:T(8,128)(2,1)S(1)}, u32[]{:S(2)}, u32[]{:S(2)}) collective-permute-start(bf16[1,512,256]{2,1,0:T(8,128)(2,1)S(1)} %fusion.61), channel_id=1, source_target_pairs={{0,16},{4,20},{8,24},{12,28},{16,0},{20,4},{24,8},{28,12},{1,17},{... | collective-permute-start | bytes 786440 | tf_op jit(solution)/shard_map/ppermute | solution.py:17
  170.1 14.2 %collective-permute-start.7 = (bf16[512,256]{1,0:T(8,128)(2,1)S(1)}, bf16[512,256]{1,0:T(8,128)(2,1)S(1)}, u32[]{:S(2)}, u32[]{:S(2)}) collective-permute-start(bf16[512,256]{1,0:T(8,128)(2,1)S(1)} %dynamic-slice_bitcast_fusion.1), channel_id=1, source_target_pairs={{0,16},{4,20},{8,24},{12,28},{16,0},{20,4},{24,8},{28,12},{1,17},{... | collective-permute-start | bytes 786440 | tf_op jit(solution)/shard_map/ppermute | solution.py:17
  184.3 3.5 copy-start.4
  205.7 2.5 copy-start.8
  219.8 2.7 copy-start.16
  221.4 2.1 copy-start.14
  224.7 193.8 %reduce-scatter.5.cloned.1.call-start = ((), (), s32[]{:S(2)}) async-start(), calls=%async_computation.5 | async-start | bytes 4718592 | tf_op jit(solution)/shard_map/reduce_scatter | solution.py:266
  224.8 2.8 copy-start.9
  224.8 3.8 copy-start.11
  231.6 2.8 copy-start.5
  242.1 28.9 %copy-start.2 = (bf16[2,128,2048]{2,1,0:T(8,128)(2,1)S(1)}, bf16[2,128,2048]{2,1,0:T(8,128)(2,1)}, u32[]{:S(2)}) copy-start(bf16[2,128,2048]{2,1,0:T(8,128)(2,1)} %cot_ref.3) | copy-start | bytes 3145732
  242.6 28.3 %collective-permute-start.8 = (bf16[1,512,256]{2,1,0:T(8,128)(2,1)S(1)}, bf16[1,512,256]{2,1,0:T(8,128)(2,1)S(1)}, u32[]{:S(2)}, u32[]{:S(2)}) collective-permute-start(bf16[1,512,256]{2,1,0:T(8,128)(2,1)S(1)} %fusion.60), channel_id=1, source_target_pairs={{0,16},{4,20},{8,24},{12,28},{16,0},{20,4},{24,8},{28,12},{1,17},{... | collective-permute-start | bytes 786440 | tf_op jit(solution)/shard_map/ppermute | solution.py:17
  278.3 12.3 %collective-permute-start.9 = (bf16[512,256]{1,0:T(8,128)(2,1)S(1)}, bf16[512,256]{1,0:T(8,128)(2,1)S(1)}, u32[]{:S(2)}, u32[]{:S(2)}) collective-permute-start(bf16[512,256]{1,0:T(8,128)(2,1)S(1)} %dynamic-slice_bitcast_fusion), channel_id=1, source_target_pairs={{0,16},{4,20},{8,24},{12,28},{16,0},{20,4},{24,8},{28,12},{1,17},{... | collective-permute-start | bytes 786440 | tf_op jit(solution)/shard_map/ppermute | solution.py:17
  309.9 2.5 copy-start.10
  316.4 2.9 copy-start.6
  324.7 2.6 copy-start.15
  (5 other events, 7.2 us)
Sparse Core Ops, SparseCore 0:
  10.7 76.0 all-gather.2
  89.5 80.5 all-gather.4
  224.8 98.2 reduce-scatter.2
  329.6 88.8 reduce-scatter.4
